TPU v7x, 512 devices: a whole 4x8x8 slice. The times are simulated.
512 devices in a mesh: src: 64 (over x, y, core), rcv: 8 (over z).
Axes of the slice: x: 4, y: 8, z: 8, core: 2. Of those that a mesh axis runs over, the one named last changes fastest.
Arguments:
- spectra: bfloat16 [256, 8, 3, 4096], P('src', 'rcv'), may hold values from -200 to 200, as said below
- home: int32 [256], replicated, may hold values from 0 to 255, as said below
- lists: int32 [64, 128], P('src'), may hold values from -1 to 255, as said below
Outputs:
- correlations: float32 [64, 128, 8, 8, 128], P('src', None, None, 'rcv')
Inputs may be any that keep to these rules, and one draw needn't show every extreme that they name: `spectra`: real parts in the first 2048 entries of the last dimension, imaginary parts in the last 2048. A permutation: block b is stored at position home[b]; position p lies on src index p // 4, in its slot p % 4. Each row lists distinct blocks followed by -1 entries, at least 64 blocks; no row lists more than 2 blocks stored on one src index, and some row lists 2 blocks from every src index.
All inputs are finite; a program needn't handle non-finite values.
Results may differ from a plain program's by a relative error of at most 0.007.
Values may be sent and summed in bfloat16 or wider, within the bound.
A program may use at most 64 MiB of HBM per device.

v0:
```python
import math

import jax
import jax.numpy as jnp
from jax import lax
from jax.sharding import PartitionSpec as P

LAGS = 128
BAND = 32


def whiten(stored):
    values = stored.astype(jnp.float32)
    full_shape = values.shape
    freq_count = full_shape[-1] // 2
    halves = values.reshape(full_shape[:-1] + (2, freq_count // BAND, BAND))
    energy = jnp.mean(
        halves[..., 0, :, :] * halves[..., 0, :, :] + halves[..., 1, :, :] * halves[..., 1, :, :],
        axis=-1,
        keepdims=True,
    )
    scaled = halves * lax.rsqrt(energy + 1e-05)[..., None, :, :]
    return scaled.reshape(full_shape).astype(jnp.bfloat16)


def dft_table(freq_count, lag_count):
    freq_ids = jnp.arange(freq_count, dtype=jnp.int32)[:, None]
    lag_ids = jnp.arange(lag_count, dtype=jnp.int32)[None, :] - lag_count // 2
    turn_count = freq_ids * lag_ids % (2 * freq_count)
    angles = turn_count.astype(jnp.float32) * (math.pi / freq_count)
    factor = 1.0 / math.sqrt(freq_count)
    cosine = jnp.cos(angles) * factor
    sine_part = jnp.sin(angles) * factor
    top_half = jnp.concatenate([cosine, sine_part], axis=1)
    low_half = jnp.concatenate([-sine_part, cosine], axis=1)
    return jnp.concatenate([top_half, low_half], axis=0).astype(jnp.bfloat16)


def correlate(source_block, received, dft_matrix):
    freq_count = source_block.shape[-1] // 2
    lag_count = dft_matrix.shape[1] // 2
    src_real = source_block[..., :freq_count].astype(jnp.float32)[None, :, None]
    src_imag = source_block[..., freq_count:].astype(jnp.float32)[None, :, None]
    rcv_real = received[..., :freq_count].astype(jnp.float32)[:, None]
    rcv_imag = received[..., freq_count:].astype(jnp.float32)[:, None]
    cross_real = src_real * rcv_real + src_imag * rcv_imag
    cross_imag = src_imag * rcv_real - src_real * rcv_imag
    cross = jnp.concatenate([cross_real, cross_imag], axis=-1).astype(jnp.bfloat16)
    signal = jnp.dot(
        cross.reshape(-1, 2 * freq_count), dft_matrix, preferred_element_type=jnp.float32
    )
    signal = signal.reshape(cross.shape[:-1] + (2 * lag_count,))
    real_part = signal[..., :lag_count]
    imag_part = signal[..., lag_count:]
    energy = real_part * real_part + imag_part * imag_part
    floor_term = 0.1 * jnp.mean(energy, axis=-1, keepdims=True) + 1e-05
    inverse = lax.rsqrt(energy + floor_term)
    coherent = (
        jnp.mean(real_part * inverse, axis=3) ** 2 + jnp.mean(imag_part * inverse, axis=3) ** 2
    )
    linear = jnp.mean(real_part, axis=3)
    return linear * coherent


def body(spectra, home, lists):
    whitened = whiten(spectra)
    source_block = lax.all_gather(whitened[0], "rcv", axis=0, tiled=True)
    list_row = lists[0]
    list_len = list_row.shape[0]
    is_valid = list_row >= 0
    position = home[jnp.where(is_valid, list_row, 0)]
    dft_matrix = dft_table(whitened.shape[-1] // 2, LAGS)
    stored = lax.all_gather(whitened, "src", axis=0, tiled=True)
    received = stored[position]
    rcv_count = received.shape[1]
    group_size = max(1, 32 // rcv_count)
    grouped = received.reshape((list_len // group_size, group_size) + received.shape[1:])

    def per_group(piece):
        return correlate(source_block, piece, dft_matrix)

    result = lax.map(per_group, grouped)
    result = result.reshape((list_len,) + result.shape[2:])
    result = result * is_valid[:, None, None, None].astype(jnp.float32)
    return result[None]


def solution(mesh):
    return jax.shard_map(
        body,
        mesh=mesh,
        in_specs=(P("src", "rcv", None, None), P(), P("src", None)),
        out_specs=P("src", None, None, "rcv", None),
        check_vma=False,
    )
```

profile of v0, /device:TPU:1, one launch (start us, length us, event | category | flops | bytes accessed | tf_op | source)
XLA Modules:
  0.0 150.1 jit_solution(14135608369017287826)
XLA Ops:
  6.5 1.1 reshape.275
  8.1 0.4 mul.250
  8.5 1.0 multiply_convert_fusion.1
  9.4 0.7 copy.11
  10.3 26.3 %all-gather = bf16[8,1,3,4096]{3,2,1,0:T(4,128)(2,1)S(1)} all-gather(bf16[1,1,3,4096]{3,2,1,0:T(4,128)(2,1)S(1)} %copy.10), channel_id=2, replica_groups=mesh['src'=64,'rcv'=8] {'rcv'}, dimensions={0}, use_global_device_ids=true | all-gather | bytes 221184 | tf_op jit(solution)/shard_map/all_gather | solution.py:67
  36.8 1.3 gather_fusion
  38.2 4.5 %fusion.20 = (bf16[2048,128]{1,0:T(8,128)(2,1)S(1)}, bf16[2048,128]{1,0:T(8,128)(2,1)S(1)}, bf16[2048,128]{1,0:T(8,128)(2,1)S(1)}) fusion(s32[128]{0:T(128)S(1)} %iota_add_fusion), kind=kLoop, calls=%fused_computation.40 | loop fusion | flops 5242880 | bytes 1573376 | tf_op jit(solution)/shard_map/convert.10
  42.7 0.2 maximum_maximum_fusion
  42.9 61.9 %all-gather.3.cloned.1.call-done = bf16[256,1,3,4096]{3,2,1,0:T(4,128)(2,1)} async-done(((bf16[4,1,3,4096]{3,2,1,0:T(4,128)(2,1)}), bf16[256,1,3,4096]{3,2,1,0:T(4,128)(2,1)}) %all-gather.3.cloned.1.call-update) | async-done | bytes 6291472 | tf_op jit(solution)/shard_map/all_gather | solution.py:73
  104.8 10.9 %gather_fusion.1 = bf16[128,3,4096]{2,1,0:T(4,128)(2,1)} fusion(bf16[256,3,4096]{2,1,0:T(4,128)(2,1)} %bitcast.58, s32[1024]{0:T(1024)S(1)} %pad_clamp_fusion), kind=kCustom, calls=%fused_computation.1 | custom fusion | bytes 6291968 | tf_op jit(solution)/shard_map/gather | solution.py:74
  115.7 26.3 %while.12 = (s32[]{:T(128)}, f32[4,32,8,1,128]{4,3,2,1,0:T(1,128)S(1)}, bf16[8,3,4096]{2,0,1:T(8,128)(2,1)S(1)}, bf16[4,32,1,3,4096]{4,3,1,2,0:T(4,128)(2,1)}, bf16[4096,256]{1,0:T(8,128)(2,1)S(1)}, /*index=5*/s32[]{:T(128)}) while((s32[]{:T(128)}, f32[4,32,8,1,128]{4,3,2,1,0:T(1,128)S(1)}, bf16[8,3,4096]{2,0,1:T(8,128)(2,1)S(1)}, ...), condition=%wide.region_6.7_spmd, body=%wide.region_1.6_spmd.sunk | while | flops 1637679872 | bytes 24719436 | solution.py:82
  115.7 1.6 %dynamic-slice_bitcast_fusion.2 = bf16[32,1,3,4096]{3,2,0,1:T(4,128)(2,1)S(1)} fusion(bf16[4,32,1,3,4096]{4,3,1,2,0:T(4,128)(2,1)} %get-tuple-element.167, s32[]{:T(128)} %get-tuple-element.158), kind=kLoop, calls=%fused_computation.10.clone.1 | loop fusion | bytes 1572868 | tf_op jit(solution)/shard_map/while/body/jit(dynamic_index_in_dim)/squeeze | solution.py:82
  117.6 2.1 %add_convert_fusion.2 = (bf16[32,8,3,2048]{3,1,2,0:T(8,128)(2,1)S(1)}, bf16[32,8,3,2048]{3,1,2,0:T(8,128)(2,1)S(1)}) fusion(f32[32,3,2048]{2,1,0:T(4,128)S(1)} %get-tuple-element.143, f32[8,3,2048]{2,0,1:T(8,128)S(1)} %get-tuple-element.144, f32[32,3,2048]{2,1,0:T(4,128)S(1)} %get-tuple-element.145, f32[8,3,2048]{2,0,1:T(8,128)S(1)} %get-tuple-element.146), kind=kLoop, calls=%fused_computation.7.clone.1 | loop fusion | flops 12582912 | bytes 8257536 | tf_op jit(solution)/shard_map/convert.2
  119.7 2.0 %fusion.34 = f32[32,8,1,3,256]{4,1,3,0,2:T(8,128)S(1)} fusion(bf16[4096,256]{1,0:T(8,128)(2,1)S(1)} %get-tuple-element.168, bf16[32,8,3,2048]{3,1,2,0:T(8,128)(2,1)S(1)} %get-tuple-element.147, bf16[32,8,3,2048]{3,1,2,0:T(8,128)(2,1)S(1)} %get-tuple-element.148), kind=kOutput, calls=%fused_computation.9.clone.1 | convolution fusion | flops 1623195648 | bytes 9175040 | tf_op jit(solution)/shard_map/while/body/eval_jaxpr/dot_general | solution.py:49
  122.3 1.6 %dynamic-slice_bitcast_fusion.2 = bf16[32,1,3,4096]{3,2,0,1:T(4,128)(2,1)S(1)} fusion(bf16[4,32,1,3,4096]{4,3,1,2,0:T(4,128)(2,1)} %get-tuple-element.167, s32[]{:T(128)} %get-tuple-element.158), kind=kLoop, calls=%fused_computation.10.clone.1 | loop fusion | bytes 1572868 | tf_op jit(solution)/shard_map/while/body/jit(dynamic_index_in_dim)/squeeze | solution.py:82
  124.2 2.1 %add_convert_fusion.2 = (bf16[32,8,3,2048]{3,1,2,0:T(8,128)(2,1)S(1)}, bf16[32,8,3,2048]{3,1,2,0:T(8,128)(2,1)S(1)}) fusion(f32[32,3,2048]{2,1,0:T(4,128)S(1)} %get-tuple-element.143, f32[8,3,2048]{2,0,1:T(8,128)S(1)} %get-tuple-element.144, f32[32,3,2048]{2,1,0:T(4,128)S(1)} %get-tuple-element.145, f32[8,3,2048]{2,0,1:T(8,128)S(1)} %get-tuple-element.146), kind=kLoop, calls=%fused_computation.7.clone.1 | loop fusion | flops 12582912 | bytes 8257536 | tf_op jit(solution)/shard_map/convert.2
  126.3 2.0 %fusion.34 = f32[32,8,1,3,256]{4,1,3,0,2:T(8,128)S(1)} fusion(bf16[4096,256]{1,0:T(8,128)(2,1)S(1)} %get-tuple-element.168, bf16[32,8,3,2048]{3,1,2,0:T(8,128)(2,1)S(1)} %get-tuple-element.147, bf16[32,8,3,2048]{3,1,2,0:T(8,128)(2,1)S(1)} %get-tuple-element.148), kind=kOutput, calls=%fused_computation.9.clone.1 | convolution fusion | flops 1623195648 | bytes 9175040 | tf_op jit(solution)/shard_map/while/body/eval_jaxpr/dot_general | solution.py:49
  128.9 1.6 %dynamic-slice_bitcast_fusion.2 = bf16[32,1,3,4096]{3,2,0,1:T(4,128)(2,1)S(1)} fusion(bf16[4,32,1,3,4096]{4,3,1,2,0:T(4,128)(2,1)} %get-tuple-element.167, s32[]{:T(128)} %get-tuple-element.158), kind=kLoop, calls=%fused_computation.10.clone.1 | loop fusion | bytes 1572868 | tf_op jit(solution)/shard_map/while/body/jit(dynamic_index_in_dim)/squeeze | solution.py:82
  130.8 2.1 %add_convert_fusion.2 = (bf16[32,8,3,2048]{3,1,2,0:T(8,128)(2,1)S(1)}, bf16[32,8,3,2048]{3,1,2,0:T(8,128)(2,1)S(1)}) fusion(f32[32,3,2048]{2,1,0:T(4,128)S(1)} %get-tuple-element.143, f32[8,3,2048]{2,0,1:T(8,128)S(1)} %get-tuple-element.144, f32[32,3,2048]{2,1,0:T(4,128)S(1)} %get-tuple-element.145, f32[8,3,2048]{2,0,1:T(8,128)S(1)} %get-tuple-element.146), kind=kLoop, calls=%fused_computation.7.clone.1 | loop fusion | flops 12582912 | bytes 8257536 | tf_op jit(solution)/shard_map/convert.2
  132.9 2.0 %fusion.34 = f32[32,8,1,3,256]{4,1,3,0,2:T(8,128)S(1)} fusion(bf16[4096,256]{1,0:T(8,128)(2,1)S(1)} %get-tuple-element.168, bf16[32,8,3,2048]{3,1,2,0:T(8,128)(2,1)S(1)} %get-tuple-element.147, bf16[32,8,3,2048]{3,1,2,0:T(8,128)(2,1)S(1)} %get-tuple-element.148), kind=kOutput, calls=%fused_computation.9.clone.1 | convolution fusion | flops 1623195648 | bytes 9175040 | tf_op jit(solution)/shard_map/while/body/eval_jaxpr/dot_general | solution.py:49
  135.5 1.6 %dynamic-slice_bitcast_fusion.2 = bf16[32,1,3,4096]{3,2,0,1:T(4,128)(2,1)S(1)} fusion(bf16[4,32,1,3,4096]{4,3,1,2,0:T(4,128)(2,1)} %get-tuple-element.167, s32[]{:T(128)} %get-tuple-element.158), kind=kLoop, calls=%fused_computation.10.clone.1 | loop fusion | bytes 1572868 | tf_op jit(solution)/shard_map/while/body/jit(dynamic_index_in_dim)/squeeze | solution.py:82
  137.4 2.1 %add_convert_fusion.2 = (bf16[32,8,3,2048]{3,1,2,0:T(8,128)(2,1)S(1)}, bf16[32,8,3,2048]{3,1,2,0:T(8,128)(2,1)S(1)}) fusion(f32[32,3,2048]{2,1,0:T(4,128)S(1)} %get-tuple-element.143, f32[8,3,2048]{2,0,1:T(8,128)S(1)} %get-tuple-element.144, f32[32,3,2048]{2,1,0:T(4,128)S(1)} %get-tuple-element.145, f32[8,3,2048]{2,0,1:T(8,128)S(1)} %get-tuple-element.146), kind=kLoop, calls=%fused_computation.7.clone.1 | loop fusion | flops 12582912 | bytes 8257536 | tf_op jit(solution)/shard_map/convert.2
  139.5 2.0 %fusion.34 = f32[32,8,1,3,256]{4,1,3,0,2:T(8,128)S(1)} fusion(bf16[4096,256]{1,0:T(8,128)(2,1)S(1)} %get-tuple-element.168, bf16[32,8,3,2048]{3,1,2,0:T(8,128)(2,1)S(1)} %get-tuple-element.147, bf16[32,8,3,2048]{3,1,2,0:T(8,128)(2,1)S(1)} %get-tuple-element.148), kind=kOutput, calls=%fused_computation.9.clone.1 | convolution fusion | flops 1623195648 | bytes 9175040 | tf_op jit(solution)/shard_map/while/body/eval_jaxpr/dot_general | solution.py:49
  142.1 1.2 bitcast_multiply_fusion
  (47 shorter events, 3.7 us)
Async XLA Ops:
  6.5 30.3 %copy-start = (s32[256]{0:T(256)S(1)}, s32[256]{0:T(256)}, u32[]{:S(2)}) copy-start(s32[256]{0:T(256)} %param.6) | copy-start | bytes 3076
  6.5 30.2 %copy-start.1 = (s32[1,128]{1,0:T(1,128)S(1)}, s32[1,128]{1,0:T(1,128)}, u32[]{:S(2)}) copy-start(s32[1,128]{1,0:T(1,128)} %param.7) | copy-start | bytes 1540
  6.5 98.3 %all-gather.3.cloned.1.call-start = ((), (), s32[]{:S(2)}) async-start(), calls=%async_computation | async-start | bytes 8519680 | tf_op jit(solution)/shard_map/all_gather | solution.py:73
Sparse Core Ops, SparseCore 0:
  10.7 94.0 all-gather.2
where the time goes:
time: 150 us
  waiting for transfers between devices  62 us (41%)
  blocking collectives  26.3 us (18%)
  local copies, waits for them, and re-layouts  21.5 us (14%)
  other arithmetic  18.4 us (12%)
  between operations  13.5 us (9%)
  matrix products  8.06 us (5%)
    all_gather x1, waiting for transfers between devices, body(): stored = lax.all_gather(whitened, 'src', axis=0, tiled=True)  61.9 us
    all_gather x1, blocking collectives, body(): source_block = lax.all_gather(whitened[0], 'rcv', axis=0, tiled=True)  26.3 us
    another operation x5, other arithmetic  12.8 us
    gather x1, local copies, waits for them, and re-layouts, body(): received = stored[position]  10.9 us
    dot_general x4, matrix products, correlate(): jnp.dot(cross.reshape(-1, 2 * freq_count), dft_matrix, preferred_element_...  8.06 us
    squeeze x4, local copies, waits for them, and re-layouts, body(): result = lax.map(per_group, grouped)  6.58 us
  transfers between devices with their start and end apart: 1, of which 1 were waited for; matrix products, arithmetic and copies ran while one was open for 4% of the time, Pallas kernels for 0%

commit v1 on v0

v1 whole, which is shorter than its diff:
```python
import functools
import math

import jax
import jax.numpy as jnp
import numpy as np
from jax import lax
from jax.experimental import pallas as pl
from jax.experimental.pallas import tpu as pltpu
from jax.sharding import PartitionSpec as P

F = 2048
LAGS = 128
W = 3
BAND = 32
LIST = 128
X = 4
FT = 512
BF = jnp.bfloat16
F32 = jnp.float32
MESH = pl.DeviceIdType.MESH


def tables():
    freq = np.arange(F, dtype=np.int64)[:, None]
    lag = np.arange(LAGS, dtype=np.int64)[None, :] - LAGS // 2
    angle = ((freq * lag) % (2 * F)).astype(np.float64) * (math.pi / F)
    dft = np.concatenate([np.cos(angle), np.sin(angle)], axis=1) / math.sqrt(F)
    sel_s = np.zeros((16, W, 8, X, 16, W), np.float32)
    for r in range(8):
        for q in range(16):
            for w in range(W):
                sel_s[q, w, r, r // 2, q, w] = 1
    sel_r = np.zeros((4, W, 8, 4, W, 4), np.float32)
    for q in range(4):
        for w in range(W):
            sel_r[q, w, :, q, w, :] = 1
    block = np.zeros((8, 4, W, 4), np.float32) + np.arange(4)[None, None, None, :]
    lanes = np.arange(128)
    band = (lanes[:, None] // BAND == lanes[None, :] // BAND) / BAND
    return (
        dft.astype(np.float32).astype(BF),
        sel_s.reshape(16 * W * 8, X * 16 * W).astype(BF),
        sel_r.reshape(4 * W * 8, 4 * 4 * W),
        block.reshape(8, 4 * 4 * W),
        band.astype(BF),
    )


def exact_dot(a, b):
    hi = a.astype(BF)
    rest = a - hi.astype(F32)
    mid = rest.astype(BF)
    low = (rest - mid.astype(F32)).astype(BF)
    dot = functools.partial(jnp.dot, preferred_element_type=F32)
    return dot(hi, b) + dot(mid, b) + dot(low, b)


def kernel(
    Y, Z,
    spec_ref, home_ref, lists_ref, dft_hbm, sel_s_ref, sel_r_ref, block_ref, band_ref,
    out_ref,
    dft, rf, sf, rbuf, sbuf, gbuf, ubuf, vbuf, rg, tbuf, obuf, ibuf, of, osel,
    dft_sem, yss, yrs, qss, qrs, xss, xrs, gss, grs, zass, zars, zbss, zbrs, bxss, bxrs,
    oss, ors,
):
    HY, HZ = Y // 2, Z // 2
    src = lax.axis_index("src")
    z = lax.axis_index("rcv")
    c = lax.rem(src, 2)
    y = lax.rem(src // 2, Y)
    x = src // (2 * Y)

    def dev(xx, yy, cc, zz):
        return ((xx * Y + yy) * 2 + cc, zz)

    def mod(a, n):
        return lax.rem(a + n, n)

    def remote(a, b, ss, rs, device):
        return pltpu.make_async_remote_copy(
            src_ref=a, dst_ref=b, send_sem=ss, recv_sem=rs, device_id=device, device_id_type=MESH
        )

    barrier = pltpu.get_barrier_semaphore()
    peers = [dev(x, y, 1 - c, z)]
    if Y > 1:
        peers += [dev(x, mod(y + 1, Y), c, z), dev(x, mod(y - 1, Y), c, z)]
    peers += [dev(mod(x + d, X), y, c, z) for d in range(1, X)]
    peers += [dev(x, y, c, mod(z + d, Z)) for d in range(1, Z)]
    for peer in peers:
        pl.semaphore_signal(barrier, inc=1, device_id=peer, device_id_type=MESH)

    load_dft = pltpu.make_async_copy(dft_hbm, dft, dft_sem)
    load_dft.start()
    if Y < 8:
        ibuf[...] = jnp.zeros_like(ibuf)
        obuf[...] = jnp.zeros_like(obuf)

    pad = jnp.zeros((4, F), F32)
    spectra, energies = [], []
    for w in range(W):
        s = spec_ref[w].astype(F32)
        spectra.append(s)
        e = s[:, :F] * s[:, :F] + s[:, F:] * s[:, F:]
        e = jnp.concatenate([e, pad], axis=0)
        energies += [e[:, t * 128 : t * 128 + 128] for t in range(16)]
    mean = exact_dot(jnp.concatenate(energies, axis=0), band_ref[...])
    scale = lax.rsqrt(mean + 1e-05)
    for w in range(W):
        for t in range(16):
            k = scale[(w * 16 + t) * 8 : (w * 16 + t) * 8 + 4]
            for part in range(2):
                v = spectra[w][:, part * F + t * 128 : part * F + t * 128 + 128] * k
                q, lane = part * 2 + t // 8, (t % 8) * 128
                rf[pl.ds(q * 12 + w * 4, 4), pl.ds(lane, 128)] = v
                sf[pl.ds(t * 3 + w, 1), pl.ds(part * 128, 128)] = v[:1]
    rbuf[c, y] = rf[...].astype(BF)
    sbuf[z, x] = sf[...].astype(BF)

    sub = lax.broadcasted_iota(jnp.int32, (128, 128), 0)
    listed = lists_ref[...]
    home = home_ref[...].astype(F32)
    pos = jnp.zeros((1, 128), F32)
    for h in range(2):
        column = jnp.transpose(jnp.broadcast_to(home[h : h + 1], (128, 128)))
        hit = listed == sub + h * 128
        pos = pos + jnp.sum(jnp.where(hit, column, 0.0), axis=0, keepdims=True)
    pos = jnp.where(listed >= 0, pos, -1.0)
    pos = jnp.transpose(jnp.broadcast_to(pos, (128, 128)))
    lane = lax.broadcasted_iota(jnp.int32, (1, 128), 1)
    lane_c = (lane >> 4) & 1
    lane_n = (lane >> 1) & 7
    lane_y = (y + jnp.where((lane_n & 1) == 1, (lane_n + 1) >> 1, Y - (lane_n >> 1))) & (Y - 1)
    base = ((((lane >> 5) * Y + lane_y) * 2 + (lane & 1)) * 4).astype(F32)
    base = jnp.where(lane_n < Y, base, -100.0)
    has = [
        jnp.max(jnp.where(pos == base + b, 1.0, 0.0), axis=0, keepdims=True) > 0.5
        for b in range(4)
    ]
    first = jnp.where(has[0], 0.0, jnp.where(has[1], 1.0, jnp.where(has[2], 2.0, 3.0)))
    last = jnp.where(has[3], 3.0, jnp.where(has[2], 2.0, jnp.where(has[1], 1.0, 0.0)))
    pick = jnp.where(lane_c == 1, last, first)
    target = jnp.where((lane_c == 1) & (first == last), -50.0, base + pick)
    osel[...] = jnp.where(pos == target, 1.0, 0.0).astype(BF)
    gbuf[x] = jnp.broadcast_to(pick, (8, 128))

    pl.semaphore_wait(barrier, len(peers))

    started = []

    def start(copy):
        copy.start()
        started.append(copy)

    def x_peer(d):
        return dev(mod(x + d, X), y, c, z)

    def y_copy(way, d, h):
        at = mod(y - d, Y) if way == 0 else mod(y + d, Y)
        to = mod(y + 1, Y) if way == 0 else mod(y - 1, Y)
        ref = rbuf.at[c, at, :, pl.ds(h * 512, 512)]
        return remote(ref, ref, yss.at[way, d, h], yrs.at[way, d, h], dev(x, to, c, z))

    def y_pieces(way, d):
        return (0, 1) if d + 1 < HY else ((way,) if d + 1 == HY else ())

    def q_copy(rel, h):
        ref = rbuf.at[c, mod(y + rel, Y), :, pl.ds(h * 512, 512)]
        return remote(ref, ref, qss.at[rel, h], qrs.at[rel, h], dev(x, y, 1 - c, z))

    def q_arrival(rel, h):
        ref = rbuf.at[1 - c, mod(y + rel, Y), :, pl.ds(h * 512, 512)]
        return remote(ref, ref, qss.at[rel, h], qrs.at[rel, h], dev(x, y, 1 - c, z))

    def xa_copy(d):
        ref = sbuf.at[z, x, :, pl.ds(0, 128)]
        return remote(ref, ref, xss.at[d - 1], xrs.at[d - 1], x_peer(d))

    def xa_arrival(d):
        ref = sbuf.at[z, mod(x - d, X), :, pl.ds(0, 128)]
        return remote(ref, ref, xss.at[d - 1], xrs.at[d - 1], x_peer(d))

    def g_copy(d):
        return remote(gbuf.at[x], gbuf.at[x], gss.at[d - 1], grs.at[d - 1], x_peer(d))

    def g_arrival(d):
        ref = gbuf.at[mod(x - d, X)]
        return remote(ref, ref, gss.at[d - 1], grs.at[d - 1], x_peer(d))

    def za_copy(way, d, arrival=False):
        to = mod(z + 1, Z) if way == 0 else mod(z - 1, Z)
        e = d + 1 if arrival else d
        at = mod(z - e, Z) if way == 0 else mod(z + e, Z)
        if d + 1 < HZ:
            ref = sbuf.at[at, :, :, pl.ds(0, 128)]
        else:
            ref = sbuf.at[at, pl.ds(way * 2, 2), :, pl.ds(0, 128)]
        return remote(ref, ref, zass.at[way, d], zars.at[way, d], dev(x, y, c, to))

    def y_arrival(way, d, h):
        e = d + 1
        at = mod(y - e, Y) if way == 0 else mod(y + e, Y)
        ref = rbuf.at[c, at, :, pl.ds(h * 512, 512)]
        return remote(ref, ref, yss.at[way, d, h], yrs.at[way, d, h], dev(x, y, 1 - c, z))

    def zb_copy(d):
        ref = sbuf.at[z, x, :, pl.ds(128, 128)]
        return remote(ref, ref, zbss.at[d - 1], zbrs.at[d - 1], dev(x, y, c, mod(z + d, Z)))

    def zb_arrival(d):
        ref = sbuf.at[mod(z - d, Z), x, :, pl.ds(128, 128)]
        return remote(ref, ref, zbss.at[d - 1], zbrs.at[d - 1], dev(x, y, c, mod(z + d, Z)))

    def bx_copy(d, rel):
        ref = sbuf.at[mod(z + rel, Z), x, :, pl.ds(128, 128)]
        return remote(ref, ref, bxss.at[d - 1, rel], bxrs.at[d - 1, rel], x_peer(d))

    def bx_arrival(d, rel):
        ref = sbuf.at[mod(z + rel, Z), mod(x - d, X), :, pl.ds(128, 128)]
        return remote(ref, ref, bxss.at[d - 1, rel], bxrs.at[d - 1, rel], x_peer(d))

    M = 2 * Z

    def o_copy(d, n):
        rows = pl.ds(pl.multiple_of(n * M, M), M)
        to = mod(x + d, X)
        return remote(
            obuf.at[to, :, rows], ibuf.at[x, :, rows], oss.at[d - 1, n], ors.at[d - 1, n], x_peer(d)
        )

    def o_arrival(d, n):
        rows = pl.ds(pl.multiple_of(n * M, M), M)
        ref = ibuf.at[mod(x - d, X), :, rows]
        return remote(ref, ref, oss.at[d - 1, n], ors.at[d - 1, n], x_peer(d))

    for d in range(1, X):
        start(xa_copy(d))
    for d in range(1, Z):
        start(zb_copy(d))
    for way in range(2):
        for h in y_pieces(way, 0):
            start(y_copy(way, 0, h))
    for d in range(1, X):
        start(g_copy(d))
    for d in range(1, X):
        start(bx_copy(d, 0))
    for h in range(2):
        start(q_copy(0, h))
    for d in range(1, X):
        xa_arrival(d).wait_recv()
    if HZ:
        for way in range(2):
            start(za_copy(way, 0))
    for d in range(1, X):
        g_arrival(d).wait_recv()

    def z_step(d):
        for way in range(2):
            if d <= HZ:
                za_copy(way, d - 1, arrival=True).wait_recv()
                if d < HZ:
                    start(za_copy(way, d))
        for e in sorted({d, Z - d}):
            if d <= HZ:
                zb_arrival(e).wait_recv()
                for k in range(1, X):
                    start(bx_copy(k, Z - e))

    def y_step(d):
        for way in range(2):
            for h in y_pieces(way, d - 1):
                y_arrival(way, d - 1, h).wait_recv()
                if h in y_pieces(way, d):
                    start(y_copy(way, d, h))
                rel = Y - d if way == 0 else d
                start(q_copy(rel, h))

    def assemble(rel):
        at = mod(z + rel, Z)
        for d in range(1, X):
            bx_arrival(d, rel).wait_recv()
        rows = jnp.dot(
            sel_s_ref[...], sbuf[at].reshape(X * 48, 256), preferred_element_type=F32
        )
        for q in range(16):
            for w in range(W):
                v = rows[(q * W + w) * 8 : (q * W + w) * 8 + 8]
                re, im = v[:, :128], v[:, 128:]
                ubuf[at, w, :, pl.ds(q * 128, 128)] = jnp.concatenate([re, im], axis=0).astype(BF)
                vbuf[at, w, :, pl.ds(q * 128, 128)] = jnp.concatenate([im, -re], axis=0).astype(BF)

    for d in range(1, max(HY, HZ + 1)):
        if d <= HZ:
            z_step(d)
        if d < HY:
            y_step(d)
        for rel in sorted({d - 1, (Z - d + 1) % Z}):
            assemble(rel)
    if HZ:
        assemble(HZ)
    elif HY <= 1:
        assemble(0)
    load_dft.wait()

    g_rows = lax.broadcasted_iota(jnp.int32, (8, 128), 0)
    g_lanes = lax.broadcasted_iota(jnp.int32, (8, 128), 1)
    picks = gbuf[0]
    for s in range(1, X):
        picks = jnp.where((g_rows >> 1) == s, gbuf[s], picks)

    @pl.loop(0, Y)
    def _(n):
        rel = jnp.where(lax.rem(n, 2) == 1, (n + 1) // 2, lax.rem(Y - n // 2, Y))
        at = mod(y + rel, Y)
        if HY:

            @pl.when(n == max(Y - 3, 0))
            def _():
                for way in range(2):
                    y_arrival(way, HY - 1, way).wait_recv()
                    q_copy(HY, way).start()

        for h in range(2):
            q_arrival(rel, h).wait_recv()

        for core in range(2):
            mark = x * 32 + (g_rows & 1) * 16 + n * 2 + core
            column = jnp.sum(jnp.where(g_lanes == mark, picks, 0.0), axis=1, keepdims=True)
            sel = jnp.where(block_ref[...] == column, 1.0, 0.0)
            sel = (jnp.concatenate([sel] * 12, axis=0) * sel_r_ref[...]).astype(BF)
            rows = jnp.dot(sel, rbuf[core, at], preferred_element_type=F32)
            for q in range(4):
                for w in range(W):
                    v = rows[(q * W + w) * 8 : (q * W + w) * 8 + 8]
                    rg[core, w, q // 2, :, pl.ds((q % 2) * 1024, 1024)] = jnp.concatenate(
                        [v, v], axis=0
                    ).astype(BF)

        signal = None
        for f in range(0, F, FT):
            fs = pl.ds(f, FT)
            rows = []
            for w in range(W):
                for core in range(2):
                    rr, ri = rg[core, w, 0, :, fs], rg[core, w, 1, :, fs]
                    for i in range(Z):
                        rows.append(ubuf[i, w, :, fs] * rr + vbuf[i, w, :, fs] * ri)
            part = jnp.dot(jnp.concatenate(rows, axis=0), dft[fs, :], preferred_element_type=F32)
            signal = part if signal is None else signal + part
        signal = signal.reshape(W, M, 2, 8, 256)
        real = signal[:, :, 0, :, :128] - signal[:, :, 1, :, 128:]
        imag = signal[:, :, 0, :, 128:] + signal[:, :, 1, :, :128]
        energy = real * real + imag * imag
        inverse = lax.rsqrt(energy + (0.1 * jnp.mean(energy, axis=-1, keepdims=True) + 1e-05))
        pr, pi = real * inverse, imag * inverse
        third = 1.0 / 3.0
        mr = (pr[0] + pr[1] + pr[2]) * third
        mi = (pi[0] + pi[1] + pi[2]) * third
        tbuf[...] = ((real[0] + real[1] + real[2]) * third) * (mr * mr + mi * mi)
        at_rows = pl.ds(pl.multiple_of(n * M, M), M)
        for s in range(X):
            for k in range(2):
                obuf[s, k, at_rows, :] = tbuf[:, 2 * s + k, :].astype(BF)
        for d in range(1, X):
            o_copy(d, n).start()

    for copy in started:
        copy.wait_send()
    if HY:
        for way in range(2):
            q_copy(HY, way).wait_send()
    ibuf[x] = obuf[x]
    for d in range(1, X):
        for n in range(Y):
            o_copy(d, n).wait_send()
            o_arrival(d, n).wait_recv()
    of[...] = ibuf[...].astype(F32).reshape(128 * Z, 128)
    for i in range(Z):
        rows = of[pl.ds(i, 128, stride=Z), :].astype(BF)
        out_ref[:, i, :] = jnp.dot(osel[...], rows, preferred_element_type=F32)


def body(spectra, home, lists, Y, Z):
    dft, sel_s, sel_r, block, band = (jnp.asarray(t) for t in tables())
    vmem = pl.BlockSpec(memory_space=pltpu.VMEM)
    dma = pltpu.SemaphoreType.DMA
    HY, HZ = max(Y // 2, 1), max(Z // 2, 1)
    out = pl.pallas_call(
        functools.partial(kernel, Y, Z),
        out_shape=jax.ShapeDtypeStruct((LIST, Z, LAGS), F32),
        in_specs=[vmem] * 3 + [pl.BlockSpec(memory_space=pl.ANY)] + [vmem] * 4,
        out_specs=vmem,
        scratch_shapes=[
            pltpu.VMEM((F, 2 * LAGS), BF),
            pltpu.VMEM((48, 1024), F32),
            pltpu.VMEM((48, 256), F32),
            pltpu.VMEM((2, Y, 48, 1024), BF),
            pltpu.VMEM((Z, X, 48, 256), BF),
            pltpu.VMEM((X, 8, 128), F32),
            pltpu.VMEM((Z, W, 16, F), BF),
            pltpu.VMEM((Z, W, 16, F), BF),
            pltpu.VMEM((2, W, 2, 16, F), BF),
            pltpu.VMEM((2 * Z, 8, 128), F32),
            pltpu.VMEM((X, 2, 16 * Z, 128), BF),
            pltpu.VMEM((X, 2, 16 * Z, 128), BF),
            pltpu.VMEM((128 * Z, 128), F32),
            pltpu.VMEM((128, 128), BF),
            dma,
            dma((2, HY, 2)), dma((2, HY, 2)),
            dma((Y, 2)), dma((Y, 2)),
            dma((X - 1,)), dma((X - 1,)),
            dma((X - 1,)), dma((X - 1,)),
            dma((2, HZ)), dma((2, HZ)),
            dma((max(Z - 1, 1),)), dma((max(Z - 1, 1),)),
            dma((X - 1, Z)), dma((X - 1, Z)),
            dma((X - 1, Y)), dma((X - 1, Y)),
        ],
        compiler_params=pltpu.CompilerParams(
            collective_id=0, has_side_effects=True, vmem_limit_bytes=48 * 2**20
        ),
        cost_estimate=pl.CostEstimate(
            flops=6_500_000_000, bytes_accessed=4_000_000, transcendentals=400_000
        ),
    )(spectra.transpose(1, 2, 0, 3)[0], home.reshape(2, 128), lists, dft, sel_s, sel_r, block, band)
    return out[None, :, :, None, :]


def solution(mesh):
    Y = mesh.shape["src"] // (2 * X)
    Z = mesh.shape["rcv"]
    return jax.shard_map(
        functools.partial(body, Y=Y, Z=Z),
        mesh=mesh,
        in_specs=(P("src", "rcv", None, None), P(), P("src", None)),
        out_specs=P("src", None, None, "rcv", None),
        check_vma=False,
    )
```

time: 150 us -> 57.6 us (0.38)
  the two profiles are of different devices: /device:TPU:1 before, /device:TPU:24 now
where the time goes in v1:
time: 57.6 us; the launch traced here: 57.3 us
  Pallas kernels  51.2 us (89%)
  local copies, waits for them, and re-layouts  6.09 us (11%)
    pallas_call x1, Pallas kernels, body(): pl.pallas_call(functools.partial(kernel, Y, Z), out_shape=jax.ShapeDtypeS...  51.2 us
    unnamed x17, local copies, waits for them, and re-layouts  6.09 us

profile of v1, /device:TPU:24, one launch (start us, length us, event | category | flops | bytes accessed | tf_op | source)
XLA Modules:
  0.0 57.3 jit_solution(6194013701913525683)
XLA Ops:
  0.0 0.0 copy-start.7
  0.0 0.0 copy-start.1
  0.0 0.0 copy-start.2
  0.0 0.7 %copy-done.7 = f32[8,48]{1,0:T(8,128)S(1)} copy-done((f32[8,48]{1,0:T(8,128)S(1)}, f32[8,48]{1,0:T(8,128)}, u32[]{:S(2)}) %copy-start.7) | copy-done | bytes 1560
  0.7 0.0 copy-done.1
  0.7 0.0 copy-done.2
  0.7 0.0 copy-start
  0.7 0.9 %copy-done = bf16[4,1,3,4096]{3,0,2,1:T(4,128)(2,1)S(1)} copy-done((bf16[4,1,3,4096]{3,0,2,1:T(4,128)(2,1)S(1)}, bf16[4,1,3,4096]{3,0,2,1:T(4,128)(2,1)}, u32[]{:S(2)}) %copy-start) | copy-done | bytes 98328
  1.6 0.0 copy-start.3
  1.6 1.2 %copy-done.3 = bf16[2048,256]{1,0:T(8,128)(2,1)S(1)} copy-done((bf16[2048,256]{1,0:T(8,128)(2,1)S(1)}, bf16[2048,256]{1,0:T(8,128)(2,1)}, u32[]{:S(2)}) %copy-start.3) | copy-done | bytes 1048600
  2.8 0.0 copy-start.4
  2.8 0.9 %copy-done.4 = bf16[384,192]{1,0:T(8,128)(2,1)S(1)} copy-done((bf16[384,192]{1,0:T(8,128)(2,1)S(1)}, bf16[384,192]{1,0:T(8,128)(2,1)}, u32[]{:S(2)}) %copy-start.4) | copy-done | bytes 147480
  3.7 0.0 copy-start.5
  3.7 0.8 %copy-done.5 = f32[96,48]{1,0:T(8,128)S(1)} copy-done((f32[96,48]{1,0:T(8,128)S(1)}, f32[96,48]{1,0:T(8,128)}, u32[]{:S(2)}) %copy-start.5) | copy-done | bytes 18456
  4.5 0.0 copy-start.6
  4.5 0.8 %copy-done.6 = bf16[128,128]{1,0:T(8,128)(2,1)S(1)} copy-done((bf16[128,128]{1,0:T(8,128)(2,1)S(1)}, bf16[128,128]{1,0:T(8,128)(2,1)}, u32[]{:S(2)}) %copy-start.6) | copy-done | bytes 32792
  5.3 51.2 %shard_map.82 = f32[128,8,128]{2,1,0:T(8,128)S(1)} custom-call(bf16[3,4,4096]{2,1,0:T(4,128)(2,1)S(1)} %bitcast.8, s32[2,128]{1,0:T(2,128)S(1)} %bitcast.9, s32[1,128]{1,0:T(1,128)S(1)} %copy-done.2, bf16[2048,256]{1,0:T(8,128)(2,1)S(1)} %copy-done.3, bf16[384,192]{1,0:T(8,128)(2,1)S(1)} %copy-done.4, f32[96,48]{1,0:T(8,128)S(1)} %copy-done.5, ...), custom_call_target="tpu_custom_call" | custom-call | flops 6499999744 | bytes 4000000 | tf_op jit(solution)/shard_map/pallas_call | solution.py:389
  56.5 0.8 %copy.11 = f32[1,128,8,1,128]{4,3,2,1,0:T(1,128)} copy(f32[1,128,8,1,128]{4,3,2,1,0:T(1,128)S(1)} %bitcast.7) | data formatting | bytes 1048576
Async XLA Ops:
  0.0 0.7 %copy-start.7 = (f32[8,48]{1,0:T(8,128)S(1)}, f32[8,48]{1,0:T(8,128)}, u32[]{:S(2)}) copy-start(f32[8,48]{1,0:T(8,128)} %constant.13.clone.block_ref) | copy-start | bytes 4612
  0.0 0.7 %copy-start.1 = (s32[256]{0:T(256)S(1)}, s32[256]{0:T(256)}, u32[]{:S(2)}) copy-start(s32[256]{0:T(256)} %param.9) | copy-start | bytes 3076
  0.0 0.7 %copy-start.2 = (s32[1,128]{1,0:T(1,128)S(1)}, s32[1,128]{1,0:T(1,128)}, u32[]{:S(2)}) copy-start(s32[1,128]{1,0:T(1,128)} %lists_ref.1) | copy-start | bytes 1540
  0.7 0.9 %copy-start = (bf16[4,1,3,4096]{3,0,2,1:T(4,128)(2,1)S(1)}, bf16[4,1,3,4096]{3,0,2,1:T(4,128)(2,1)}, u32[]{:S(2)}) copy-start(bf16[4,1,3,4096]{3,0,2,1:T(4,128)(2,1)} %param.8) | copy-start | bytes 294916
  1.6 1.2 %copy-start.3 = (bf16[2048,256]{1,0:T(8,128)(2,1)S(1)}, bf16[2048,256]{1,0:T(8,128)(2,1)}, u32[]{:S(2)}) copy-start(bf16[2048,256]{1,0:T(8,128)(2,1)} %constant.10.clone.dft_hbm) | copy-start | bytes 3145732
  2.8 0.9 %copy-start.4 = (bf16[384,192]{1,0:T(8,128)(2,1)S(1)}, bf16[384,192]{1,0:T(8,128)(2,1)}, u32[]{:S(2)}) copy-start(bf16[384,192]{1,0:T(8,128)(2,1)} %constant.11.clone.sel_s_ref) | copy-start | bytes 442372
  3.7 0.8 %copy-start.5 = (f32[96,48]{1,0:T(8,128)S(1)}, f32[96,48]{1,0:T(8,128)}, u32[]{:S(2)}) copy-start(f32[96,48]{1,0:T(8,128)} %constant.12.clone.sel_r_ref) | copy-start | bytes 55300
  4.5 0.8 %copy-start.6 = (bf16[128,128]{1,0:T(8,128)(2,1)S(1)}, bf16[128,128]{1,0:T(8,128)(2,1)}, u32[]{:S(2)}) copy-start(bf16[128,128]{1,0:T(8,128)(2,1)} %constant.14.clone.band_ref) | copy-start | bytes 98308

commit v2 on v1

v2 whole, which is shorter than its diff:
```python
import functools
import math

import jax
import jax.numpy as jnp
import numpy as np
from jax import lax
from jax.experimental import pallas as pl
from jax.experimental.pallas import tpu as pltpu
from jax.sharding import PartitionSpec as P

F = 2048
LAGS = 128
W = 3
BAND = 32
LIST = 128
X = 4
FT = 512
BF = jnp.bfloat16
F32 = jnp.float32
MESH = pl.DeviceIdType.MESH


def tables():
    freq = np.arange(F, dtype=np.int64)[:, None]
    lag = np.arange(LAGS, dtype=np.int64)[None, :] - LAGS // 2
    angle = ((freq * lag) % (2 * F)).astype(np.float64) * (math.pi / F)
    dft = np.concatenate([np.cos(angle), np.sin(angle)], axis=1) / math.sqrt(F)
    sel_s = np.zeros((16, W, 8, X, 16, W), np.float32)
    for r in range(8):
        for q in range(16):
            for w in range(W):
                sel_s[q, w, r, r // 2, q, w] = 1
    sel_r = np.zeros((4, W, 8, 4, W, 4), np.float32)
    for q in range(4):
        for w in range(W):
            sel_r[q, w, :, q, w, :] = 1
    block = np.zeros((8, 4, W, 4), np.float32) + np.arange(4)[None, None, None, :]
    lanes = np.arange(128)
    band = (lanes[:, None] // BAND == lanes[None, :] // BAND) / BAND
    return (
        dft.astype(np.float32).astype(BF),
        sel_s.reshape(16 * W * 8, X * 16 * W).astype(BF),
        sel_r.reshape(4 * W * 8, 4 * 4 * W),
        block.reshape(8, 4 * 4 * W),
        band.astype(BF),
    )


def exact_dot(a, b):
    hi = a.astype(BF)
    rest = a - hi.astype(F32)
    mid = rest.astype(BF)
    low = (rest - mid.astype(F32)).astype(BF)
    dot = functools.partial(jnp.dot, preferred_element_type=F32)
    return dot(hi, b) + dot(mid, b) + dot(low, b)


def kernel(
    Y, Z,
    spec_hbm, home_hbm, lists_hbm, dft_hbm, sel_s_hbm, sel_r_hbm, block_hbm, band_hbm,
    out_ref,
    spec_ref, home_ref, lists_ref, dft, sel_s_ref, sel_r_ref, block_ref, band_ref,
    rf, sf, rbuf, sbuf, gbuf, ubuf, vbuf, rg, tbuf, obuf, ibuf, of, osel,
    in_sem, yss, yrs, qss, qrs, gss, grs, nss, nrs, zss, zrs, xss, xrs, oss, ors,
):
    HY, HZ = Y // 2, Z // 2
    src = lax.axis_index("src")
    z = lax.axis_index("rcv")
    c = lax.rem(src, 2)
    y = lax.rem(src // 2, Y)
    x = src // (2 * Y)
    order = [0]
    for d in range(1, HZ + 1):
        order += sorted({d, Z - d})

    def dev(xx, yy, cc, zz):
        return ((xx * Y + yy) * 2 + cc, zz)

    def mod(a, n):
        return lax.rem(a + n, n)

    def remote(a, b, ss, rs, device):
        return pltpu.make_async_remote_copy(
            src_ref=a, dst_ref=b, send_sem=ss, recv_sem=rs, device_id=device, device_id_type=MESH
        )

    barrier = pltpu.get_barrier_semaphore()
    peers = [dev(x, y, 1 - c, z)]
    peers += [dev(x, mod(y + 1, Y), c, z), dev(x, mod(y - 1, Y), c, z)]
    peers += [dev(mod(x + d, X), y, c, z) for d in range(1, X)]
    peers += [dev(x, y, c, mod(z + d, Z)) for d in range(1, Z)]
    for peer in peers:
        pl.semaphore_signal(barrier, inc=1, device_id=peer, device_id_type=MESH)

    loads = [
        pltpu.make_async_copy(a, b, in_sem.at[k])
        for k, (a, b) in enumerate((
            (spec_hbm, spec_ref), (band_hbm, band_ref), (home_hbm, home_ref),
            (lists_hbm, lists_ref), (sel_s_hbm, sel_s_ref), (sel_r_hbm, sel_r_ref),
            (block_hbm, block_ref), (dft_hbm, dft),
        ))
    ]
    for load in loads:
        load.start()
    if Y < 8:
        ibuf[...] = jnp.zeros_like(ibuf)
        obuf[...] = jnp.zeros_like(obuf)
    loads[0].wait()
    loads[1].wait()

    pad = jnp.zeros((4, F), F32)
    spectra, energies = [], []
    for w in range(W):
        s = spec_ref[w].astype(F32)
        spectra.append(s)
        e = s[:, :F] * s[:, :F] + s[:, F:] * s[:, F:]
        e = jnp.concatenate([e, pad], axis=0)
        energies += [e[:, t * 128 : t * 128 + 128] for t in range(16)]
    mean = exact_dot(jnp.concatenate(energies, axis=0), band_ref[...])
    scale = lax.rsqrt(mean + 1e-05)
    for w in range(W):
        for t in range(16):
            k = scale[(w * 16 + t) * 8 : (w * 16 + t) * 8 + 4]
            for part in range(2):
                v = spectra[w][:, part * F + t * 128 : part * F + t * 128 + 128] * k
                q, lane = part * 2 + t // 8, (t % 8) * 128
                rf[pl.ds(q * 12 + w * 4, 4), pl.ds(lane, 128)] = v
                sf[part, pl.ds(t * 3 + w, 1), :] = v[:1]
    whitened = rf[...].astype(BF)
    for h in range(2):
        rbuf[c, y, h] = whitened[:, h * 512 : h * 512 + 512]
    sbuf[z, x] = sf[...].astype(BF)

    pl.semaphore_wait(barrier, len(peers))

    started = []

    def start(copy):
        copy.start()
        started.append(copy)

    def x_peer(d):
        return dev(mod(x + d, X), y, c, z)

    def y_copy(way, d, h, arrival=False):
        e = d + 1 if arrival else d
        at = mod(y - e, Y) if way == 0 else mod(y + e, Y)
        to = mod(y + 1, Y) if way == 0 else mod(y - 1, Y)
        ref = rbuf.at[c, at, h]
        return remote(ref, ref, yss.at[way, d, h], yrs.at[way, d, h], dev(x, to, c, z))

    def y_pieces(way, d):
        return (0, 1) if d + 1 < HY else ((way,) if d + 1 == HY else ())

    def q_copy(rel, h, core):
        ref = rbuf.at[core, mod(y + rel, Y), h]
        return remote(ref, ref, qss.at[rel, h], qrs.at[rel, h], dev(x, y, 1 - c, z))

    def g_copy(d, origin):
        ref = gbuf.at[origin]
        return remote(ref, ref, gss.at[d - 1], grs.at[d - 1], x_peer(d))

    def z_copy(d, origin):
        ref = sbuf.at[origin, x]
        return remote(ref, ref, zss.at[d - 1], zrs.at[d - 1], dev(x, y, c, mod(z + d, Z)))

    def near_copy(way, origin):
        to = mod(z + 1, Z) if way == 0 else mod(z - 1, Z)
        ref = sbuf.at[origin]
        return remote(ref, ref, nss.at[way], nrs.at[way], dev(x, y, c, to))

    def x_copy(d, rel, origin):
        ref = sbuf.at[mod(z + rel, Z), origin]
        return remote(ref, ref, xss.at[d - 1, rel], xrs.at[d - 1, rel], x_peer(d))

    M = 2 * Z

    def o_copy(d, t, arrival=False):
        rows = pl.ds(pl.multiple_of(t * M, M), M)
        a = ibuf.at[mod(x - d, X), :, rows] if arrival else obuf.at[mod(x + d, X), :, rows]
        b = ibuf.at[mod(x - d, X) if arrival else x, :, rows]
        return remote(a, b, oss.at[d - 1, t], ors.at[d - 1, t], x_peer(d))

    near = (1, Z - 1) if Z > 2 else ()
    far = [d for d in order[1:] if d not in near]
    for d in far:
        start(z_copy(d, z))
    for d in range(1, X):
        start(x_copy(d, 0, x))
    for way in range(2):
        for h in y_pieces(way, 0):
            start(y_copy(way, 0, h))
    for h in range(2):
        start(q_copy(0, h, c))

    for load in loads[2:]:
        load.wait()
    sub = lax.broadcasted_iota(jnp.int32, (128, 128), 0)
    listed = lists_ref[...]
    home = home_ref[...].astype(F32)
    pos = jnp.zeros((1, 128), F32)
    for h in range(2):
        column = jnp.transpose(jnp.broadcast_to(home[h : h + 1], (128, 128)))
        hit = listed == sub + h * 128
        pos = pos + jnp.sum(jnp.where(hit, column, 0.0), axis=0, keepdims=True)
    pos = jnp.where(listed >= 0, pos, -1.0)
    pos = jnp.transpose(jnp.broadcast_to(pos, (128, 128)))
    lane = lax.broadcasted_iota(jnp.int32, (1, 128), 1)
    lane_c = (lane >> 4) & 1
    lane_n = (lane >> 1) & 7
    lane_y = (y + jnp.where((lane_n & 1) == 1, (lane_n + 1) >> 1, Y - (lane_n >> 1))) & (Y - 1)
    base = ((((lane >> 5) * Y + lane_y) * 2 + (lane & 1)) * 4).astype(F32)
    base = jnp.where(lane_n < Y, base, -100.0)
    has = [
        jnp.max(jnp.where(pos == base + b, 1.0, 0.0), axis=0, keepdims=True) > 0.5
        for b in range(4)
    ]
    first = jnp.where(has[0], 0.0, jnp.where(has[1], 1.0, jnp.where(has[2], 2.0, 3.0)))
    last = jnp.where(has[3], 3.0, jnp.where(has[2], 2.0, jnp.where(has[1], 1.0, 0.0)))
    pick = jnp.where(lane_c == 1, last, first)
    target = jnp.where((lane_c == 1) & (first == last), -50.0, base + pick)
    osel[...] = jnp.where(pos == target, 1.0, 0.0).astype(BF)
    gbuf[x] = jnp.broadcast_to(pick, (8, 128))

    for d in range(1, X):
        start(g_copy(d, x))

    def z_step(rel):
        z_copy(Z - rel, mod(z + rel, Z)).wait_recv()
        for k in range(1, X):
            start(x_copy(k, rel, x))

    def y_step(d, send):
        for way in range(2):
            for h in y_pieces(way, d - 1):
                y_copy(way, d - 1, h, arrival=True).wait_recv()
                if h in y_pieces(way, d):
                    send(y_copy(way, d, h))
                send(q_copy(Y - d if way == 0 else d, h, c))

    def assemble(k):
        rel = order[k]
        at = mod(z + rel, Z)
        if rel in near:
            near_copy(near.index(rel) ^ 1, at).wait_recv()
        elif rel:
            for d in range(1, X):
                x_copy(d, rel, mod(x - d, X)).wait_recv()
        parts = sbuf[at]
        parts = jnp.concatenate(
            [parts[:, 0].reshape(X * 48, 128), parts[:, 1].reshape(X * 48, 128)], axis=1
        )
        rows = jnp.dot(sel_s_ref[...], parts, preferred_element_type=F32)
        for q in range(16):
            for w in range(W):
                v = rows[(q * W + w) * 8 : (q * W + w) * 8 + 8]
                re, im = v[:, :128], v[:, 128:]
                ubuf[k, w, :, pl.ds(q * 128, 128)] = jnp.concatenate([re, im], axis=0).astype(BF)
                vbuf[k, w, :, pl.ds(q * 128, 128)] = jnp.concatenate([im, -re], axis=0).astype(BF)

    NM = HY
    for d in range(1, X):
        x_copy(d, 0, mod(x - d, X)).wait_recv()
    if near:
        for way in range(2):
            start(near_copy(way, z))
    if HY > 1:
        y_step(1, start)
    assemble(0)
    if HY > 2:
        y_step(2, start)
    for rel in far:
        z_step(rel)
    for k in range(1, HZ):
        assemble(k)
    for d in range(1, X):
        g_copy(d, mod(x - d, X)).wait_recv()

    g_rows = lax.broadcasted_iota(jnp.int32, (8, 128), 0)
    g_lanes = lax.broadcasted_iota(jnp.int32, (8, 128), 1)
    picks = gbuf[0]
    for s in range(1, X):
        picks = jnp.where((g_rows >> 1) == s, gbuf[s], picks)

    def begin(copy):
        copy.start()

    second = NM - 1 if NM > 1 else 1

    @pl.loop(0, 2 * NM)
    def _(t):
        half = jnp.where(t < NM - 1, 0, jnp.where(t < 2 * NM - 2, 1, t - (2 * NM - 2)))
        m = jnp.where(t < NM - 1, t, jnp.where(t < 2 * NM - 2, t - (NM - 1), NM - 1))
        if HY > 3:

            @pl.when(t == 1)
            def _():
                y_step(3, begin)

        @pl.when(t == max(2 * NM - 5, 0))
        def _():
            y_step(HY, begin)

        @pl.when(t == second)
        def _():
            for k in range(HZ, Z):
                assemble(k)

        @pl.when(half == 0)
        def _():
            for u in range(2):
                n = 2 * m + u
                rel = jnp.where(u == 1, m + 1, lax.rem(Y - m, Y))
                at = mod(y + rel, Y)
                for h in range(2):
                    q_copy(rel, h, 1 - c).wait_recv()
                for core in range(2):
                    mark = x * 32 + (g_rows & 1) * 16 + n * 2 + core
                    column = jnp.sum(jnp.where(g_lanes == mark, picks, 0.0), axis=1, keepdims=True)
                    sel = jnp.where(block_ref[...] == column, 1.0, 0.0)
                    sel = (jnp.concatenate([sel] * 12, axis=0) * sel_r_ref[...]).astype(BF)
                    for h in range(2):
                        rows = jnp.dot(sel, rbuf[core, at, h], preferred_element_type=F32)
                        for q in range(4):
                            for w in range(W):
                                v = rows[(q * W + w) * 8 : (q * W + w) * 8 + 8]
                                rg[2 * n + core, w, q // 2, :, pl.ds((q % 2) * 1024 + h * 512, 512)] = (
                                    jnp.concatenate([v, v], axis=0).astype(BF)
                                )

        signal = None
        for f in range(0, F, FT):
            fs = pl.ds(f, FT)
            rows = []
            for w in range(W):
                for u in range(4):
                    rr, ri = rg[4 * m + u, w, 0, :, fs], rg[4 * m + u, w, 1, :, fs]
                    for k in range(HZ):
                        i = half * HZ + k
                        rows.append(ubuf[i, w, :, fs] * rr + vbuf[i, w, :, fs] * ri)
            part = jnp.dot(jnp.concatenate(rows, axis=0), dft[fs, :], preferred_element_type=F32)
            signal = part if signal is None else signal + part
        signal = signal.reshape(W, M, 2, 8, 256)
        real = signal[:, :, 0, :, :128] - signal[:, :, 1, :, 128:]
        imag = signal[:, :, 0, :, 128:] + signal[:, :, 1, :, :128]
        energy = real * real + imag * imag
        inverse = lax.rsqrt(energy + (0.1 * jnp.mean(energy, axis=-1, keepdims=True) + 1e-05))
        pr, pi = real * inverse, imag * inverse
        third = 1.0 / 3.0
        mr = (pr[0] + pr[1] + pr[2]) * third
        mi = (pi[0] + pi[1] + pi[2]) * third
        tbuf[...] = ((real[0] + real[1] + real[2]) * third) * (mr * mr + mi * mi)
        slot = m * 2 + half
        at_rows = pl.ds(pl.multiple_of(slot * M, M), M)
        for s in range(X):
            for k in range(2):
                obuf[s, k, at_rows, :] = tbuf[:, 2 * s + k, :].astype(BF)
        for d in range(1, X):
            o_copy(d, slot).start()

    for copy in started:
        copy.wait_send()
    for d in sorted({HY, 3} if HY > 3 else {HY}):
        for way in range(2):
            for h in y_pieces(way, d - 1):
                if h in y_pieces(way, d):
                    y_copy(way, d, h).wait_send()
                q_copy(Y - d if way == 0 else d, h, c).wait_send()
    ibuf[x] = obuf[x]
    for d in range(1, X):
        for t in range(2 * NM):
            o_copy(d, t).wait_send()
            o_copy(d, t, arrival=True).wait_recv()
    of[...] = ibuf[...].astype(F32).reshape(X * 2 * 8 * 2 * Z, 128)
    for k in range(Z):
        rows = []
        for block in range(X * 2 * 4):
            rows.append(of[pl.ds(block * 4 * Z + (k // HZ) * 2 * Z + k % HZ, 4, stride=HZ), :])
        rows = jnp.concatenate(rows, axis=0).astype(BF)
        out_ref[:, pl.ds(mod(z + order[k], Z), 1), :] = jnp.dot(
            osel[...], rows, preferred_element_type=F32
        )[:, None, :]


def body(spectra, home, lists, Y, Z):
    dft, sel_s, sel_r, block, band = (jnp.asarray(t) for t in tables())
    vmem = pl.BlockSpec(memory_space=pltpu.VMEM)
    dma = pltpu.SemaphoreType.DMA
    HY = Y // 2
    out = pl.pallas_call(
        functools.partial(kernel, Y, Z),
        out_shape=jax.ShapeDtypeStruct((LIST, Z, LAGS), F32),
        in_specs=[pl.BlockSpec(memory_space=pl.ANY)] * 8,
        out_specs=vmem,
        scratch_shapes=[
            pltpu.VMEM((W, 4, 2 * F), BF),
            pltpu.VMEM((2, 128), jnp.int32),
            pltpu.VMEM((1, LIST), jnp.int32),
            pltpu.VMEM(dft.shape, BF),
            pltpu.VMEM(sel_s.shape, BF),
            pltpu.VMEM(sel_r.shape, F32),
            pltpu.VMEM(block.shape, F32),
            pltpu.VMEM(band.shape, BF),
            pltpu.VMEM((48, 1024), F32),
            pltpu.VMEM((2, 48, 128), F32),
            pltpu.VMEM((2, Y, 2, 48, 512), BF),
            pltpu.VMEM((Z, X, 2, 48, 128), BF),
            pltpu.VMEM((X, 8, 128), F32),
            pltpu.VMEM((Z, W, 16, F), BF),
            pltpu.VMEM((Z, W, 16, F), BF),
            pltpu.VMEM((2 * Y, W, 2, 16, F), BF),
            pltpu.VMEM((2 * Z, 8, 128), F32),
            pltpu.VMEM((X, 2, 16 * Z, 128), BF),
            pltpu.VMEM((X, 2, 16 * Z, 128), BF),
            pltpu.VMEM((128 * Z, 128), F32),
            pltpu.VMEM((128, 128), BF),
            dma((8,)),
            dma((2, HY, 2)), dma((2, HY, 2)),
            dma((Y, 2)), dma((Y, 2)),
            dma((X - 1,)), dma((X - 1,)),
            dma((2,)), dma((2,)),
            dma((Z - 1,)), dma((Z - 1,)),
            dma((X - 1, Z)), dma((X - 1, Z)),
            dma((X - 1, Y)), dma((X - 1, Y)),
        ],
        compiler_params=pltpu.CompilerParams(
            collective_id=0, has_side_effects=True, vmem_limit_bytes=60 * 2**20
        ),
        cost_estimate=pl.CostEstimate(
            flops=6_500_000_000, bytes_accessed=4_000_000, transcendentals=400_000
        ),
    )(spectra.transpose(1, 2, 0, 3)[0], home.reshape(2, 128), lists, dft, sel_s, sel_r, block, band)
    return out[None, :, :, None, :]


def solution(mesh):
    Y = mesh.shape["src"] // (2 * X)
    Z = mesh.shape["rcv"]
    return jax.shard_map(
        functools.partial(body, Y=Y, Z=Z),
        mesh=mesh,
        in_specs=(P("src", "rcv", None, None), P(), P("src", None)),
        out_specs=P("src", None, None, "rcv", None),
        check_vma=False,
    )
```

time: 57.6 us -> 47.1 us (0.82)
  the two profiles are of different devices: /device:TPU:24 before, /device:TPU:1 now
where the time goes in v2:
time: 47.1 us; the launch traced here: 46.6 us
  Pallas kernels  44.7 us (95%)
  local copies, waits for them, and re-layouts  1.87 us (4%)
    pallas_call x1, Pallas kernels, body(): pl.pallas_call(functools.partial(kernel, Y, Z), out_shape=jax.ShapeDtypeS...  44.7 us
    unnamed x1, local copies, waits for them, and re-layouts  1.87 us

profile of v2, /device:TPU:1, one launch (start us, length us, event | category | flops | bytes accessed | tf_op | source)
XLA Modules:
  0.0 46.6 jit_solution(8534198039335904477)
XLA Ops:
  0.0 44.7 %shard_map.82 = f32[128,8,128]{2,1,0:T(8,128)} custom-call(bf16[3,4,4096]{2,1,0:T(4,128)(2,1)} %bitcast.8, s32[2,128]{1,0:T(2,128)} %bitcast.9, s32[1,128]{1,0:T(1,128)} %lists_hbm.1, bf16[2048,256]{1,0:T(8,128)(2,1)} %constant.10.clone.dft_hbm, bf16[384,192]{1,0:T(8,128)(2,1)} %constant.11.clone.sel_s_hbm, f32[96,48]{1,0:T(8,128)} %constant.12.clone.sel_r_hbm, ...), custom_call_target="tpu_custom_call" | custom-call | flops 6499999744 | bytes 4000000 | tf_op jit(solution)/shard_map/pallas_call | solution.py:391
  44.7 1.9 %copy.11 = f32[1,128,8,1,128]{4,3,2,1,0:T(1,128)} copy(f32[1,128,8,1,128]{4,3,2,1,0:T(1,128)} %bitcast.7) | data formatting | bytes 1048576

commit v3 on v2

--- a/solution.py
+++ b/solution.py
@@ -15,7 +15,7 @@
 BAND = 32
 LIST = 128
 X = 4
-FT = 512
+FT = 2048
 BF = jnp.bfloat16
 F32 = jnp.float32
 MESH = pl.DeviceIdType.MESH
@@ -61,7 +61,7 @@
     spec_hbm, home_hbm, lists_hbm, dft_hbm, sel_s_hbm, sel_r_hbm, block_hbm, band_hbm,
     out_ref,
     spec_ref, home_ref, lists_ref, dft, sel_s_ref, sel_r_ref, block_ref, band_ref,
-    rf, sf, rbuf, sbuf, gbuf, ubuf, vbuf, rg, tbuf, obuf, ibuf, of, osel,
+    rf, sf, rbuf, sbuf, gbuf, ubuf, vbuf, rg, tbuf, rbuf32, obuf, ibuf, of, osel,
     in_sem, yss, yrs, qss, qrs, gss, grs, nss, nrs, zss, zrs, xss, xrs, oss, ors,
 ):
     HY, HZ = Y // 2, Z // 2
@@ -174,13 +174,14 @@
         ref = sbuf.at[mod(z + rel, Z), origin]
         return remote(ref, ref, xss.at[d - 1, rel], xrs.at[d - 1, rel], x_peer(d))
 
-    M = 2 * Z
-
-    def o_copy(d, t, arrival=False):
-        rows = pl.ds(pl.multiple_of(t * M, M), M)
+    GZ = Z // 4
+    M = 4 * GZ
+
+    def o_copy(d, m, arrival=False):
+        rows = pl.ds(pl.multiple_of(m * 4 * Z, 4 * Z), 4 * Z)
         a = ibuf.at[mod(x - d, X), :, rows] if arrival else obuf.at[mod(x + d, X), :, rows]
         b = ibuf.at[mod(x - d, X) if arrival else x, :, rows]
-        return remote(a, b, oss.at[d - 1, t], ors.at[d - 1, t], x_peer(d))
+        return remote(a, b, oss.at[d - 1, m], ors.at[d - 1, m], x_peer(d))
 
     near = (1, Z - 1) if Z > 2 else ()
     far = [d for d in order[1:] if d not in near]
@@ -260,19 +261,18 @@
                 vbuf[k, w, :, pl.ds(q * 128, 128)] = jnp.concatenate([im, -re], axis=0).astype(BF)
 
     NM = HY
+    steps = [(0, 0), (0, 1), (1, 0), (1, 1), (2, 0), (2, 1), (0, 2), (1, 2), (2, 2)]
+    steps += [(3, 0), (3, 1), (3, 2)] + [(g, 3) for g in range(4)]
     for d in range(1, X):
         x_copy(d, 0, mod(x - d, X)).wait_recv()
-    if near:
-        for way in range(2):
-            start(near_copy(way, z))
-    if HY > 1:
-        y_step(1, start)
+    for way in range(2):
+        start(near_copy(way, z))
+    y_step(1, start)
     assemble(0)
-    if HY > 2:
-        y_step(2, start)
     for rel in far:
         z_step(rel)
-    for k in range(1, HZ):
+    y_step(2, start)
+    for k in range(1, GZ):
         assemble(k)
     for d in range(1, X):
         g_copy(d, mod(x - d, X)).wait_recv()
@@ -286,28 +286,26 @@
     def begin(copy):
         copy.start()
 
-    second = NM - 1 if NM > 1 else 1
-
-    @pl.loop(0, 2 * NM)
+    @pl.loop(0, len(steps))
     def _(t):
-        half = jnp.where(t < NM - 1, 0, jnp.where(t < 2 * NM - 2, 1, t - (2 * NM - 2)))
-        m = jnp.where(t < NM - 1, t, jnp.where(t < 2 * NM - 2, t - (NM - 1), NM - 1))
-        if HY > 3:
-
-            @pl.when(t == 1)
-            def _():
-                y_step(3, begin)
-
-        @pl.when(t == max(2 * NM - 5, 0))
-        def _():
-            y_step(HY, begin)
-
-        @pl.when(t == second)
-        def _():
-            for k in range(HZ, Z):
-                assemble(k)
-
-        @pl.when(half == 0)
+        group = m = 0
+        for k, (g, at) in enumerate(steps):
+            group = jnp.where(t == k, g, group)
+            m = jnp.where(t == k, at, m)
+        for d, when in ((3, 3), (4, 8)):
+
+            @pl.when(t == when)
+            def _(d=d):
+                y_step(d, begin)
+
+        for g in range(1, 4):
+
+            @pl.when(t == steps.index((g, 0)))
+            def _(g=g):
+                for k in range(g * GZ, g * GZ + GZ):
+                    assemble(k)
+
+        @pl.when(group == 0)
         def _():
             for u in range(2):
                 n = 2 * m + u
@@ -336,8 +334,8 @@
             for w in range(W):
                 for u in range(4):
                     rr, ri = rg[4 * m + u, w, 0, :, fs], rg[4 * m + u, w, 1, :, fs]
-                    for k in range(HZ):
-                        i = half * HZ + k
+                    for k in range(GZ):
+                        i = group * GZ + k
                         rows.append(ubuf[i, w, :, fs] * rr + vbuf[i, w, :, fs] * ri)
             part = jnp.dot(jnp.concatenate(rows, axis=0), dft[fs, :], preferred_element_type=F32)
             signal = part if signal is None else signal + part
@@ -351,13 +349,19 @@
         mr = (pr[0] + pr[1] + pr[2]) * third
         mi = (pi[0] + pi[1] + pi[2]) * third
         tbuf[...] = ((real[0] + real[1] + real[2]) * third) * (mr * mr + mi * mi)
-        slot = m * 2 + half
-        at_rows = pl.ds(pl.multiple_of(slot * M, M), M)
+        at_rows = pl.ds(pl.multiple_of(m * 4 * Z + group * M, M), M)
         for s in range(X):
             for k in range(2):
-                obuf[s, k, at_rows, :] = tbuf[:, 2 * s + k, :].astype(BF)
-        for d in range(1, X):
-            o_copy(d, slot).start()
+                rbuf32[s, k, at_rows, :] = tbuf[:, 2 * s + k, :]
+
+        @pl.when(group == 3)
+        def _():
+            all_rows = pl.ds(pl.multiple_of(m * 4 * Z, 4 * Z), 4 * Z)
+            for s in range(X):
+                for k in range(2):
+                    obuf[s, k, all_rows, :] = rbuf32[s, k, all_rows, :].astype(BF)
+            for d in range(1, X):
+                o_copy(d, m).start()
 
     for copy in started:
         copy.wait_send()
@@ -369,14 +373,14 @@
                 q_copy(Y - d if way == 0 else d, h, c).wait_send()
     ibuf[x] = obuf[x]
     for d in range(1, X):
-        for t in range(2 * NM):
-            o_copy(d, t).wait_send()
-            o_copy(d, t, arrival=True).wait_recv()
+        for m in range(NM):
+            o_copy(d, m).wait_send()
+            o_copy(d, m, arrival=True).wait_recv()
     of[...] = ibuf[...].astype(F32).reshape(X * 2 * 8 * 2 * Z, 128)
     for k in range(Z):
         rows = []
         for block in range(X * 2 * 4):
-            rows.append(of[pl.ds(block * 4 * Z + (k // HZ) * 2 * Z + k % HZ, 4, stride=HZ), :])
+            rows.append(of[pl.ds(block * 4 * Z + (k // GZ) * M + k % GZ, 4, stride=GZ), :])
         rows = jnp.concatenate(rows, axis=0).astype(BF)
         out_ref[:, pl.ds(mod(z + order[k], Z), 1), :] = jnp.dot(
             osel[...], rows, preferred_element_type=F32
@@ -410,7 +414,8 @@
             pltpu.VMEM((Z, W, 16, F), BF),
             pltpu.VMEM((Z, W, 16, F), BF),
             pltpu.VMEM((2 * Y, W, 2, 16, F), BF),
-            pltpu.VMEM((2 * Z, 8, 128), F32),
+            pltpu.VMEM((Z, 8, 128), F32),
+            pltpu.VMEM((X, 2, 16 * Z, 128), F32),
             pltpu.VMEM((X, 2, 16 * Z, 128), BF),
             pltpu.VMEM((X, 2, 16 * Z, 128), BF),
             pltpu.VMEM((128 * Z, 128), F32),
@@ -422,7 +427,7 @@
             dma((2,)), dma((2,)),
             dma((Z - 1,)), dma((Z - 1,)),
             dma((X - 1, Z)), dma((X - 1, Z)),
-            dma((X - 1, Y)), dma((X - 1, Y)),
+            dma((X - 1, Y // 2)), dma((X - 1, Y // 2)),
         ],
         compiler_params=pltpu.CompilerParams(
             collective_id=0, has_side_effects=True, vmem_limit_bytes=60 * 2**20

time: 47.1 us -> 46.1 us (0.979)
  Pallas kernels: 44.7 us -> 43.7 us
    pallas_call x1, Pallas kernels: 44.7 us -> 43.7 us  [body(): pl.pallas_call(functools.partial(kernel, Y, Z), out_shape=jax.ShapeDtypeS...]
where the time goes in v3:
time: 46.1 us; the launch traced here: 45.6 us
  Pallas kernels  43.7 us (95%)
  local copies, waits for them, and re-layouts  1.87 us (4%)
    pallas_call x1, Pallas kernels, body(): pl.pallas_call(functools.partial(kernel, Y, Z), out_shape=jax.ShapeDtypeS...  43.7 us
    unnamed x1, local copies, waits for them, and re-layouts  1.87 us

profile of v3, /device:TPU:1, one launch (start us, length us, event | category | flops | bytes accessed | tf_op | source)
XLA Modules:
  0.0 45.6 jit_solution(9266172502920692588)
XLA Ops:
  0.0 43.7 %shard_map.82 = f32[128,8,128]{2,1,0:T(8,128)} custom-call(bf16[3,4,4096]{2,1,0:T(4,128)(2,1)} %bitcast.8, s32[2,128]{1,0:T(2,128)} %bitcast.9, s32[1,128]{1,0:T(1,128)} %lists_hbm.1, bf16[2048,256]{1,0:T(8,128)(2,1)} %constant.10.clone.dft_hbm, bf16[384,192]{1,0:T(8,128)(2,1)} %constant.11.clone.sel_s_hbm, f32[96,48]{1,0:T(8,128)} %constant.12.clone.sel_r_hbm, ...), custom_call_target="tpu_custom_call" | custom-call | flops 6499999744 | bytes 4000000 | tf_op jit(solution)/shard_map/pallas_call | solution.py:395
  43.7 1.9 %copy.11 = f32[1,128,8,1,128]{4,3,2,1,0:T(1,128)} copy(f32[1,128,8,1,128]{4,3,2,1,0:T(1,128)} %bitcast.7) | data formatting | bytes 1048576

commit v4 on v3

--- a/solution.py
+++ b/solution.py
@@ -261,8 +261,8 @@
                 vbuf[k, w, :, pl.ds(q * 128, 128)] = jnp.concatenate([im, -re], axis=0).astype(BF)
 
     NM = HY
-    steps = [(0, 0), (0, 1), (1, 0), (1, 1), (2, 0), (2, 1), (0, 2), (1, 2), (2, 2)]
-    steps += [(3, 0), (3, 1), (3, 2)] + [(g, 3) for g in range(4)]
+    steps = [(0, 0), (0, 1), (1, 0), (1, 1), (2, 0), (2, 1), (3, 0), (3, 1)]
+    steps += [(g, 2) for g in range(4)] + [(g, 3) for g in range(4)]
     for d in range(1, X):
         x_copy(d, 0, mod(x - d, X)).wait_recv()
     for way in range(2):
@@ -292,7 +292,7 @@
         for k, (g, at) in enumerate(steps):
             group = jnp.where(t == k, g, group)
             m = jnp.where(t == k, at, m)
-        for d, when in ((3, 3), (4, 8)):
+        for d, when in ((3, 4), (4, 9)):
 
             @pl.when(t == when)
             def _(d=d):

time: 46.1 us -> 46.1 us (level)
  no operation moved by 1% of the time
where the time goes in v4:
time: 46.1 us; the launch traced here: 45.6 us
  Pallas kernels  43.7 us (95%)
  local copies, waits for them, and re-layouts  1.87 us (4%)
    pallas_call x1, Pallas kernels, body(): pl.pallas_call(functools.partial(kernel, Y, Z), out_shape=jax.ShapeDtypeS...  43.7 us
    unnamed x1, local copies, waits for them, and re-layouts  1.87 us

profile of v4, /device:TPU:1, one launch (start us, length us, event | category | flops | bytes accessed | tf_op | source)
XLA Modules:
  0.0 45.6 jit_solution(16987872443627233595)
XLA Ops:
  0.0 43.7 %shard_map.82 = f32[128,8,128]{2,1,0:T(8,128)} custom-call(bf16[3,4,4096]{2,1,0:T(4,128)(2,1)} %bitcast.8, s32[2,128]{1,0:T(2,128)} %bitcast.9, s32[1,128]{1,0:T(1,128)} %lists_hbm.1, bf16[2048,256]{1,0:T(8,128)(2,1)} %constant.10.clone.dft_hbm, bf16[384,192]{1,0:T(8,128)(2,1)} %constant.11.clone.sel_s_hbm, f32[96,48]{1,0:T(8,128)} %constant.12.clone.sel_r_hbm, ...), custom_call_target="tpu_custom_call" | custom-call | flops 6499999744 | bytes 4000000 | tf_op jit(solution)/shard_map/pallas_call | solution.py:395
  43.7 1.9 %copy.11 = f32[1,128,8,1,128]{4,3,2,1,0:T(1,128)} copy(f32[1,128,8,1,128]{4,3,2,1,0:T(1,128)} %bitcast.7) | data formatting | bytes 1048576
